TPU v7x, 512 devices: a whole 4x4x16 slice. The times are simulated.
512 devices in a mesh: mode: 32 (over y, z_hi, x), rows: 16 (over z_lo, core).
Axes of the slice: x: 4, y: 4, z: 16 (z_hi: 2, z_lo: 8; z = z_hi * 8 + z_lo), core: 2. Of those that a mesh axis runs over, the one named last changes fastest.
Arguments:
- tangents: float32 [128, 3, 128, 1024], P('mode', None, 'rows'), may hold values from -6 to 6
- checkpoints: float32 [8, 3, 128, 1024], P(None, None, 'rows', 'mode'), may hold values from 0 to 0.5
- owner_order: int32 [8], replicated, may hold values from 0 to 7, each once
- land_mask: int32 [128, 1024], P('rows'), may hold values 0 or 1
- coefficients: float32 [128, 128], replicated, may hold values from -0.9 to 0.9
Outputs:
- vectors: float32 [128, 3, 128, 1024], P(None, None, 'rows', 'mode')
Inputs may be any that keep to these rules, and one draw needn't show every extreme that they name: `owner_order`: every checkpoint slot is named by exactly one step.
All inputs are finite; a program needn't handle non-finite values. No bound on the sum of `land_mask` on one device may be relied on, other than what follows from the above.
Results may differ from a plain program's by a relative error of at most 0.0002.
Values sent between devices are 32-bit elements; how exact they have to be, the bound alone decides.
No kernel may reach another device: no remote copies, remote signals or barrier semaphores. Data moves between devices by JAX's collectives and lax.ppermute only.
A program may use at most 64 MiB of HBM per device.

v0:
```python
import jax
import jax.numpy as jnp
from jax import lax
from jax.sharding import PartitionSpec as P

mean_depth = 1.0
gravity = 1.0
coriolis = 0.5
time_step = 0.5


def padded(cells, sides, width):
    for axis, dim in sides:
        count = lax.axis_size(axis)
        ends = count - 1
        head = lax.slice_in_dim(cells, 0, width, axis=dim)
        tail = lax.slice_in_dim(cells, cells.shape[dim] - width, cells.shape[dim], axis=dim)
        cells = jnp.concatenate(
            [
                lax.ppermute(tail, axis, [(i, (i + 1) % count) for i in range(ends)]),
                cells,
                lax.ppermute(head, axis, [((i + 1) % count, i) for i in range(ends)]),
            ],
            axis=dim,
        )
    return cells


def deriv_x(values):
    return 0.5 * (jnp.roll(values, -1, -1) - jnp.roll(values, 1, -1))


def deriv_y(values):
    return 0.5 * (values[..., 2:, :] - values[..., :-2, :])


def interior(values):
    return values[..., 1:-1, :]


def tendency(base_flow, current):
    depth_total = mean_depth + base_flow[0]
    flow_u = base_flow[1]
    flow_v = base_flow[2]
    height = current[:, 0]
    zonal = current[:, 1]
    meridional = current[:, 2]
    flux_x = depth_total * zonal + height * flow_u
    flux_y = depth_total * meridional + height * flow_v
    height_rate = -(interior(deriv_x(flux_x)) + deriv_y(flux_y))
    zonal_mid = interior(zonal)
    merid_mid = interior(meridional)
    flow_umid = interior(flow_u)
    flow_vmid = interior(flow_v)
    zonal_rate = (
        -(
            flow_umid * interior(deriv_x(zonal))
            + zonal_mid * interior(deriv_x(flow_u))
            + flow_vmid * deriv_y(zonal)
            + merid_mid * deriv_y(flow_u)
        )
        + coriolis * merid_mid
        - gravity * interior(deriv_x(height))
    )
    merid_rate = (
        -(
            flow_umid * interior(deriv_x(meridional))
            + zonal_mid * interior(deriv_x(flow_v))
            + flow_vmid * deriv_y(meridional)
            + merid_mid * deriv_y(flow_v)
        )
        - coriolis * zonal_mid
        - gravity * deriv_y(height)
    )
    return jnp.stack([height_rate, zonal_rate, merid_rate], 1)


def on_device(tangents, checkpoints, owner_order, land_mask, coefficients):
    wet_mask = land_mask.astype(jnp.float32)
    current = wet_mask * tangents
    depth = 1
    flows_wide, wet_stack = (
        padded(checkpoints, (("rows", 2),), depth),
        padded(wet_mask[None, None], (("rows", 2),), depth),
    )

    def fetch_flow(step_index):
        held_tile = lax.dynamic_index_in_dim(flows_wide, owner_order[step_index], 0, keepdims=False)
        return lax.all_gather(held_tile, "mode", axis=2, tiled=True)

    total_steps = owner_order.shape[0]

    def advance(step_index, current):
        base_wide = fetch_flow(step_index)
        widened = padded(current, (("rows", 2),), 1)
        slope_one = tendency(base_wide, widened)
        middle = wet_mask * (current + time_step * slope_one)
        middle_wide = padded(middle, (("rows", 2),), 1)
        slope_two = tendency(base_wide, middle_wide)
        return wet_mask * (current + 0.5 * time_step * (slope_one + slope_two))

    final = lax.fori_loop(0, total_steps, advance, current)
    mixing = jnp.eye(coefficients.shape[0], dtype=jnp.float32) + jnp.triu(coefficients)
    cell_block = lax.all_to_all(final, "mode", split_axis=3, concat_axis=0, tiled=True)
    flattened = cell_block.reshape(cell_block.shape[0], -1)
    mixed = jnp.dot(
        mixing.T, flattened, precision=lax.Precision.HIGHEST, preferred_element_type=jnp.float32
    )
    return mixed.reshape(cell_block.shape)


def solution(mesh):
    placed = (
        P("mode", None, "rows", None),
        P(None, None, "rows", "mode"),
        P(),
        P("rows", None),
        P(),
    )
    return jax.shard_map(
        on_device,
        mesh=mesh,
        in_specs=placed,
        out_specs=P(None, None, "rows", "mode"),
        check_vma=False,
    )
```

profile of v0, /device:TPU:97, one launch (start us, length us, event | category | flops | bytes accessed | tf_op | source)
XLA Modules:
  0.0 1700.1 jit_solution(5932026285515117026)
XLA Ops:
  0.9 5.3 collective-permute-start.4
  13.1 1625.2 %while.13 = (s32[]{:T(128)}, f32[4,3,8,1024]{3,2,1,0:T(8,128)S(1)}, f32[8,1024]{1,0:T(8,128)}, s32[8]{0:T(128)}, f32[8,3,10,32]{3,0,2,1:T(8,128)}, /*index=5*/s32[]{:T(128)}, s32[]{:T(128)}, s32[]{:T(128)}) while((s32[]{:T(128)}, f32[4,3,8,1024]{3,2,1,0:T(8,128)S(1)}, f32[8,1024]{1,0:T(8,128)}, s32[8]{0:T(128)}, f32[8,3,10,32]{3,0,2,1:T(8,128)}, ...), condition=%wide.region_1.2_spmd, body=%wide.region_0.1_spmd.sunk | while | flops 5195781 | bytes 25504440 | solution.py:102
  15.8 4.9 collective-permute-start.1
  24.9 165.8 %all-gather.2 = f32[1,3,10,1024]{2,0,1,3:T(1,128)S(1)} all-gather(f32[1,3,10,32]{2,0,1,3:T(1,128)S(1)} %copy.138), channel_id=2, replica_groups=mesh['mode'=32,'rows'=16] {'mode'}, dimensions={3}, use_global_device_ids=true | all-gather | bytes 126720 | tf_op jit(solution)/shard_map/while/body/eval_jaxpr/all_gather | solution.py:89
  204.9 16.6 collective-permute-start.2
  221.5 29.6 %collective-permute-start.3 = (f32[4,3,1,1024]{3,2,0,1:T(1,128)S(1)}, f32[4,3,1,1024]{3,2,0,1:T(1,128)S(1)}, u32[]{:S(2)}, u32[]{:S(2)}) collective-permute-start(f32[4,3,1,1024]{3,2,0,1:T(1,128)S(1)} %get-tuple-element.330), channel_id=1, source_target_pairs={{0,1},{1,2},{2,3},{3,4},{4,5},{5,6},{6,7},{7,8},{8,9},{9,10},{10,1... | collective-permute-start | bytes 147464 | tf_op jit(solution)/shard_map/while/body/eval_jaxpr/ppermute | solution.py:20
  256.8 5.5 collective-permute-start.1
  266.5 151.1 %all-gather.2 = f32[1,3,10,1024]{2,0,1,3:T(1,128)S(1)} all-gather(f32[1,3,10,32]{2,0,1,3:T(1,128)S(1)} %copy.138), channel_id=2, replica_groups=mesh['mode'=32,'rows'=16] {'mode'}, dimensions={3}, use_global_device_ids=true | all-gather | bytes 126720 | tf_op jit(solution)/shard_map/while/body/eval_jaxpr/all_gather | solution.py:89
  431.8 7.8 collective-permute-start.2
  439.6 15.1 collective-permute-start.3
  460.4 5.6 collective-permute-start.1
  470.2 151.9 %all-gather.2 = f32[1,3,10,1024]{2,0,1,3:T(1,128)S(1)} all-gather(f32[1,3,10,32]{2,0,1,3:T(1,128)S(1)} %copy.138), channel_id=2, replica_groups=mesh['mode'=32,'rows'=16] {'mode'}, dimensions={3}, use_global_device_ids=true | all-gather | bytes 126720 | tf_op jit(solution)/shard_map/while/body/eval_jaxpr/all_gather | solution.py:89
  636.3 11.9 collective-permute-start.2
  653.9 4.2 collective-permute-start
  665.4 150.4 %all-gather.2 = f32[1,3,10,1024]{2,0,1,3:T(1,128)S(1)} all-gather(f32[1,3,10,32]{2,0,1,3:T(1,128)S(1)} %copy.138), channel_id=2, replica_groups=mesh['mode'=32,'rows'=16] {'mode'}, dimensions={3}, use_global_device_ids=true | all-gather | bytes 126720 | tf_op jit(solution)/shard_map/while/body/eval_jaxpr/all_gather | solution.py:89
  830.2 10.3 collective-permute-start.2
  857.7 161.2 %all-gather.2 = f32[1,3,10,1024]{2,0,1,3:T(1,128)S(1)} all-gather(f32[1,3,10,32]{2,0,1,3:T(1,128)S(1)} %copy.138), channel_id=2, replica_groups=mesh['mode'=32,'rows'=16] {'mode'}, dimensions={3}, use_global_device_ids=true | all-gather | bytes 126720 | tf_op jit(solution)/shard_map/while/body/eval_jaxpr/all_gather | solution.py:89
  1033.1 8.1 collective-permute-start.2
  1046.9 4.2 collective-permute-start
  1058.5 153.6 %all-gather.2 = f32[1,3,10,1024]{2,0,1,3:T(1,128)S(1)} all-gather(f32[1,3,10,32]{2,0,1,3:T(1,128)S(1)} %copy.138), channel_id=2, replica_groups=mesh['mode'=32,'rows'=16] {'mode'}, dimensions={3}, use_global_device_ids=true | all-gather | bytes 126720 | tf_op jit(solution)/shard_map/while/body/eval_jaxpr/all_gather | solution.py:89
  1226.4 9.9 collective-permute-start.2
  1242.0 4.2 collective-permute-start
  1253.5 162.1 %all-gather.2 = f32[1,3,10,1024]{2,0,1,3:T(1,128)S(1)} all-gather(f32[1,3,10,32]{2,0,1,3:T(1,128)S(1)} %copy.138), channel_id=2, replica_groups=mesh['mode'=32,'rows'=16] {'mode'}, dimensions={3}, use_global_device_ids=true | all-gather | bytes 126720 | tf_op jit(solution)/shard_map/while/body/eval_jaxpr/all_gather | solution.py:89
  1429.9 4.6 collective-permute-start.2
  1452.0 155.2 %all-gather.2 = f32[1,3,10,1024]{2,0,1,3:T(1,128)S(1)} all-gather(f32[1,3,10,32]{2,0,1,3:T(1,128)S(1)} %copy.138), channel_id=2, replica_groups=mesh['mode'=32,'rows'=16] {'mode'}, dimensions={3}, use_global_device_ids=true | all-gather | bytes 126720 | tf_op jit(solution)/shard_map/while/body/eval_jaxpr/all_gather | solution.py:89
  1621.4 6.3 collective-permute-start.2
  1627.8 7.6 collective-permute-start.3
  1638.4 4.6 copy.94
  1642.9 9.3 reshape.31
  1656.3 24.8 %all-to-all-done = f32[32,1,3072]{2,1,0:T(1,128)S(1)} async-done(((f32[32,1,3072]{2,1,0:T(1,128)}), f32[32,1,3072]{2,1,0:T(1,128)S(1)}, u32[]{:S(2)}, u32[]{:S(2)}) %all-to-all-start) | async-done | bytes 393248 | tf_op jit(solution)/shard_map/all_to_all | solution.py:104
  1683.2 9.2 reshape.32
  1692.4 5.6 copy.95
  (570 shorter events, 216.0 us)
Async XLA Ops:
  0.9 9.7 collective-permute-start.4
  6.3 6.2 collective-permute-start.5
  13.9 188.2 %collective-permute-start = (f32[4,3,1,1024]{3,2,0,1:T(1,128)}, f32[4,3,1,1024]{3,2,0,1:T(1,128)}, u32[]{:S(2)}, u32[]{:S(2)}) collective-permute-start(f32[4,3,1,1024]{3,2,0,1:T(1,128)} %get-tuple-element.286), channel_id=1, source_target_pairs={{1,0},{2,1},{3,2},{4,3},{5,4},{6,5},{7,6},{8,7},{9,8},{10,9},{11,1... | collective-permute-start | bytes 147464 | tf_op jit(solution)/shard_map/while/body/eval_jaxpr/ppermute | solution.py:22
  15.8 186.2 %collective-permute-start.1 = (f32[4,3,1,1024]{3,2,0,1:T(1,128)}, f32[4,3,1,1024]{3,2,0,1:T(1,128)}, u32[]{:S(2)}, u32[]{:S(2)}) collective-permute-start(f32[4,3,1,1024]{3,2,0,1:T(1,128)} %get-tuple-element.287), channel_id=1, source_target_pairs={{0,1},{1,2},{2,3},{3,4},{4,5},{5,6},{6,7},{7,8},{8,9},{9,10},{10,1... | collective-permute-start | bytes 147464 | tf_op jit(solution)/shard_map/while/body/eval_jaxpr/ppermute | solution.py:20
  204.9 46.2 %collective-permute-start.2 = (f32[4,3,1,1024]{3,2,0,1:T(1,128)S(1)}, f32[4,3,1,1024]{3,2,0,1:T(1,128)S(1)}, u32[]{:S(2)}, u32[]{:S(2)}) collective-permute-start(f32[4,3,1,1024]{3,2,0,1:T(1,128)S(1)} %get-tuple-element.329), channel_id=1, source_target_pairs={{1,0},{2,1},{3,2},{4,3},{5,4},{6,5},{7,6},{8,7},{9,8},{10,9},{11,1... | collective-permute-start | bytes 147464 | tf_op jit(solution)/shard_map/while/body/eval_jaxpr/ppermute | solution.py:22
  221.5 30.8 %collective-permute-start.3 = (f32[4,3,1,1024]{3,2,0,1:T(1,128)S(1)}, f32[4,3,1,1024]{3,2,0,1:T(1,128)S(1)}, u32[]{:S(2)}, u32[]{:S(2)}) collective-permute-start(f32[4,3,1,1024]{3,2,0,1:T(1,128)S(1)} %get-tuple-element.330), channel_id=1, source_target_pairs={{0,1},{1,2},{2,3},{3,4},{4,5},{5,6},{6,7},{7,8},{8,9},{9,10},{10,1... | collective-permute-start | bytes 147464 | tf_op jit(solution)/shard_map/while/body/eval_jaxpr/ppermute | solution.py:20
  254.9 174.1 %collective-permute-start = (f32[4,3,1,1024]{3,2,0,1:T(1,128)}, f32[4,3,1,1024]{3,2,0,1:T(1,128)}, u32[]{:S(2)}, u32[]{:S(2)}) collective-permute-start(f32[4,3,1,1024]{3,2,0,1:T(1,128)} %get-tuple-element.286), channel_id=1, source_target_pairs={{1,0},{2,1},{3,2},{4,3},{5,4},{6,5},{7,6},{8,7},{9,8},{10,9},{11,1... | collective-permute-start | bytes 147464 | tf_op jit(solution)/shard_map/while/body/eval_jaxpr/ppermute | solution.py:22
  256.8 172.2 %collective-permute-start.1 = (f32[4,3,1,1024]{3,2,0,1:T(1,128)}, f32[4,3,1,1024]{3,2,0,1:T(1,128)}, u32[]{:S(2)}, u32[]{:S(2)}) collective-permute-start(f32[4,3,1,1024]{3,2,0,1:T(1,128)} %get-tuple-element.287), channel_id=1, source_target_pairs={{0,1},{1,2},{2,3},{3,4},{4,5},{5,6},{6,7},{7,8},{8,9},{9,10},{10,1... | collective-permute-start | bytes 147464 | tf_op jit(solution)/shard_map/while/body/eval_jaxpr/ppermute | solution.py:20
  431.8 22.9 %collective-permute-start.2 = (f32[4,3,1,1024]{3,2,0,1:T(1,128)S(1)}, f32[4,3,1,1024]{3,2,0,1:T(1,128)S(1)}, u32[]{:S(2)}, u32[]{:S(2)}) collective-permute-start(f32[4,3,1,1024]{3,2,0,1:T(1,128)S(1)} %get-tuple-element.329), channel_id=1, source_target_pairs={{1,0},{2,1},{3,2},{4,3},{5,4},{6,5},{7,6},{8,7},{9,8},{10,9},{11,1... | collective-permute-start | bytes 147464 | tf_op jit(solution)/shard_map/while/body/eval_jaxpr/ppermute | solution.py:22
  439.6 16.3 collective-permute-start.3
  458.4 175.0 %collective-permute-start = (f32[4,3,1,1024]{3,2,0,1:T(1,128)}, f32[4,3,1,1024]{3,2,0,1:T(1,128)}, u32[]{:S(2)}, u32[]{:S(2)}) collective-permute-start(f32[4,3,1,1024]{3,2,0,1:T(1,128)} %get-tuple-element.286), channel_id=1, source_target_pairs={{1,0},{2,1},{3,2},{4,3},{5,4},{6,5},{7,6},{8,7},{9,8},{10,9},{11,1... | collective-permute-start | bytes 147464 | tf_op jit(solution)/shard_map/while/body/eval_jaxpr/ppermute | solution.py:22
  460.4 173.1 %collective-permute-start.1 = (f32[4,3,1,1024]{3,2,0,1:T(1,128)}, f32[4,3,1,1024]{3,2,0,1:T(1,128)}, u32[]{:S(2)}, u32[]{:S(2)}) collective-permute-start(f32[4,3,1,1024]{3,2,0,1:T(1,128)} %get-tuple-element.287), channel_id=1, source_target_pairs={{0,1},{1,2},{2,3},{3,4},{4,5},{5,6},{6,7},{7,8},{8,9},{9,10},{10,1... | collective-permute-start | bytes 147464 | tf_op jit(solution)/shard_map/while/body/eval_jaxpr/ppermute | solution.py:20
  636.3 13.8 collective-permute-start.2
  648.2 3.1 collective-permute-start.3
  653.9 173.4 %collective-permute-start = (f32[4,3,1,1024]{3,2,0,1:T(1,128)}, f32[4,3,1,1024]{3,2,0,1:T(1,128)}, u32[]{:S(2)}, u32[]{:S(2)}) collective-permute-start(f32[4,3,1,1024]{3,2,0,1:T(1,128)} %get-tuple-element.286), channel_id=1, source_target_pairs={{1,0},{2,1},{3,2},{4,3},{5,4},{6,5},{7,6},{8,7},{9,8},{10,9},{11,1... | collective-permute-start | bytes 147464 | tf_op jit(solution)/shard_map/while/body/eval_jaxpr/ppermute | solution.py:22
  658.1 169.2 %collective-permute-start.1 = (f32[4,3,1,1024]{3,2,0,1:T(1,128)}, f32[4,3,1,1024]{3,2,0,1:T(1,128)}, u32[]{:S(2)}, u32[]{:S(2)}) collective-permute-start(f32[4,3,1,1024]{3,2,0,1:T(1,128)} %get-tuple-element.287), channel_id=1, source_target_pairs={{0,1},{1,2},{2,3},{3,4},{4,5},{5,6},{6,7},{7,8},{8,9},{9,10},{10,1... | collective-permute-start | bytes 147464 | tf_op jit(solution)/shard_map/while/body/eval_jaxpr/ppermute | solution.py:20
  830.2 12.2 collective-permute-start.2
  846.1 184.1 %collective-permute-start = (f32[4,3,1,1024]{3,2,0,1:T(1,128)}, f32[4,3,1,1024]{3,2,0,1:T(1,128)}, u32[]{:S(2)}, u32[]{:S(2)}) collective-permute-start(f32[4,3,1,1024]{3,2,0,1:T(1,128)} %get-tuple-element.286), channel_id=1, source_target_pairs={{1,0},{2,1},{3,2},{4,3},{5,4},{6,5},{7,6},{8,7},{9,8},{10,9},{11,1... | collective-permute-start | bytes 147464 | tf_op jit(solution)/shard_map/while/body/eval_jaxpr/ppermute | solution.py:22
  850.3 179.9 %collective-permute-start.1 = (f32[4,3,1,1024]{3,2,0,1:T(1,128)}, f32[4,3,1,1024]{3,2,0,1:T(1,128)}, u32[]{:S(2)}, u32[]{:S(2)}) collective-permute-start(f32[4,3,1,1024]{3,2,0,1:T(1,128)} %get-tuple-element.287), channel_id=1, source_target_pairs={{0,1},{1,2},{2,3},{3,4},{4,5},{5,6},{6,7},{7,8},{8,9},{9,10},{10,1... | collective-permute-start | bytes 147464 | tf_op jit(solution)/shard_map/while/body/eval_jaxpr/ppermute | solution.py:20
  1033.1 10.0 collective-permute-start.2
  1046.9 176.6 %collective-permute-start = (f32[4,3,1,1024]{3,2,0,1:T(1,128)}, f32[4,3,1,1024]{3,2,0,1:T(1,128)}, u32[]{:S(2)}, u32[]{:S(2)}) collective-permute-start(f32[4,3,1,1024]{3,2,0,1:T(1,128)} %get-tuple-element.286), channel_id=1, source_target_pairs={{1,0},{2,1},{3,2},{4,3},{5,4},{6,5},{7,6},{8,7},{9,8},{10,9},{11,1... | collective-permute-start | bytes 147464 | tf_op jit(solution)/shard_map/while/body/eval_jaxpr/ppermute | solution.py:22
  1051.1 172.4 %collective-permute-start.1 = (f32[4,3,1,1024]{3,2,0,1:T(1,128)}, f32[4,3,1,1024]{3,2,0,1:T(1,128)}, u32[]{:S(2)}, u32[]{:S(2)}) collective-permute-start(f32[4,3,1,1024]{3,2,0,1:T(1,128)} %get-tuple-element.287), channel_id=1, source_target_pairs={{0,1},{1,2},{2,3},{3,4},{4,5},{5,6},{6,7},{7,8},{8,9},{9,10},{10,1... | collective-permute-start | bytes 147464 | tf_op jit(solution)/shard_map/while/body/eval_jaxpr/ppermute | solution.py:20
  1226.4 11.8 collective-permute-start.2
  1242.0 185.0 %collective-permute-start = (f32[4,3,1,1024]{3,2,0,1:T(1,128)}, f32[4,3,1,1024]{3,2,0,1:T(1,128)}, u32[]{:S(2)}, u32[]{:S(2)}) collective-permute-start(f32[4,3,1,1024]{3,2,0,1:T(1,128)} %get-tuple-element.286), channel_id=1, source_target_pairs={{1,0},{2,1},{3,2},{4,3},{5,4},{6,5},{7,6},{8,7},{9,8},{10,9},{11,1... | collective-permute-start | bytes 147464 | tf_op jit(solution)/shard_map/while/body/eval_jaxpr/ppermute | solution.py:22
  1246.2 180.8 %collective-permute-start.1 = (f32[4,3,1,1024]{3,2,0,1:T(1,128)}, f32[4,3,1,1024]{3,2,0,1:T(1,128)}, u32[]{:S(2)}, u32[]{:S(2)}) collective-permute-start(f32[4,3,1,1024]{3,2,0,1:T(1,128)} %get-tuple-element.287), channel_id=1, source_target_pairs={{0,1},{1,2},{2,3},{3,4},{4,5},{5,6},{6,7},{7,8},{8,9},{9,10},{10,1... | collective-permute-start | bytes 147464 | tf_op jit(solution)/shard_map/while/body/eval_jaxpr/ppermute | solution.py:20
  1429.9 6.8 collective-permute-start.2
  1434.5 3.3 collective-permute-start.3
  1440.4 178.2 %collective-permute-start = (f32[4,3,1,1024]{3,2,0,1:T(1,128)}, f32[4,3,1,1024]{3,2,0,1:T(1,128)}, u32[]{:S(2)}, u32[]{:S(2)}) collective-permute-start(f32[4,3,1,1024]{3,2,0,1:T(1,128)} %get-tuple-element.286), channel_id=1, source_target_pairs={{1,0},{2,1},{3,2},{4,3},{5,4},{6,5},{7,6},{8,7},{9,8},{10,9},{11,1... | collective-permute-start | bytes 147464 | tf_op jit(solution)/shard_map/while/body/eval_jaxpr/ppermute | solution.py:22
  1444.4 174.1 %collective-permute-start.1 = (f32[4,3,1,1024]{3,2,0,1:T(1,128)}, f32[4,3,1,1024]{3,2,0,1:T(1,128)}, u32[]{:S(2)}, u32[]{:S(2)}) collective-permute-start(f32[4,3,1,1024]{3,2,0,1:T(1,128)} %get-tuple-element.287), channel_id=1, source_target_pairs={{0,1},{1,2},{2,3},{3,4},{4,5},{5,6},{6,7},{7,8},{8,9},{9,10},{10,1... | collective-permute-start | bytes 147464 | tf_op jit(solution)/shard_map/while/body/eval_jaxpr/ppermute | solution.py:20
  1621.4 13.9 collective-permute-start.2
  1627.8 8.8 collective-permute-start.3
  1652.3 28.8 %all-to-all-start = ((f32[32,1,3072]{2,1,0:T(1,128)}), f32[32,1,3072]{2,1,0:T(1,128)S(1)}, u32[]{:S(2)}, u32[]{:S(2)}) async-start(f32[32,1,3072]{2,1,0:T(1,128)} %reshape.31), calls=%async_computation | async-start | bytes 786432 | tf_op jit(solution)/shard_map/all_to_all | solution.py:104
  (37 other events, 71.5 us)
where the time goes:
time: 1700 us
  blocking collectives  1250 us (74%)
  starting transfers between devices  207 us (12%)
  local copies, waits for them, and re-layouts  139 us (8%)
  other arithmetic  47.6 us (3%)
  waiting for transfers between devices  36 us (2%)
  loops' own time  17.7 us (1%)
    all_gather x8, blocking collectives, fetch_flow(): return lax.all_gather(held_tile, 'mode', axis=2, tiled=True)  1250 us
    ppermute x17, starting transfers between devices, padded(): lax.ppermute(head, axis, [((i + 1) % count, i) for i in range(ends)])  104 us
    ppermute x17, starting transfers between devices, padded(): lax.ppermute(tail, axis, [(i, (i + 1) % count) for i in range(ends)])  99.2 us
    slice x208, local copies, waits for them, and re-layouts, deriv_x(): return 0.5 * (jnp.roll(values, -1, -1) - jnp.roll(values, 1, -1))  49.1 us
  transfers between devices with their start and end apart: 35, of which 10 were waited for; matrix products, arithmetic and copies ran while one was open for 7% of the time, Pallas kernels for 0%

commit v1 on v0

--- a/solution.py
+++ b/solution.py
@@ -7,6 +7,13 @@
 gravity = 1.0
 coriolis = 0.5
 time_step = 0.5
+
+
+def swapped_in(shard, axis, along):
+    size = lax.axis_size(axis)
+    pieces = jnp.stack([shard for _ in range(size)])
+    pieces = lax.all_to_all(pieces, axis, split_axis=0, concat_axis=0)
+    return jnp.concatenate(pieces, axis=along)
 
 
 def padded(cells, sides, width):
@@ -86,7 +93,7 @@
 
     def fetch_flow(step_index):
         held_tile = lax.dynamic_index_in_dim(flows_wide, owner_order[step_index], 0, keepdims=False)
-        return lax.all_gather(held_tile, "mode", axis=2, tiled=True)
+        return swapped_in(held_tile, "mode", 2)
 
     total_steps = owner_order.shape[0]
 

time: 1700 us -> 586 us (0.34)
  blocking collectives: 1250 us -> 0 us
  waiting for transfers between devices: 36 us -> 136 us
  starting transfers between devices: 207 us -> 169 us
  local copies, waits for them, and re-layouts: 139 us -> 175 us
  other arithmetic: 47.6 us -> 80.8 us
    all_gather x8 -> x0, blocking collectives: 1250 us -> none  [fetch_flow(): return lax.all_gather(held_tile, 'mode', axis=2, tiled=True)]
    all_to_all x0 -> x8, waiting for transfers between devices: none -> 104 us  [swapped_in(): pieces = lax.all_to_all(pieces, axis, split_axis=0, concat_axis=0)]
    ppermute x17, starting transfers between devices: 104 us -> 32.8 us  [padded(): lax.ppermute(head, axis, [((i + 1) % count, i) for i in range(ends)])]
    all_to_all x0 -> x8, starting transfers between devices: none -> 42.8 us  [swapped_in(): pieces = lax.all_to_all(pieces, axis, split_axis=0, concat_axis=0)]
    mul x0 -> x32, local copies, waits for them, and re-layouts: none -> 32.4 us  [the longest x16 16.1 us: deriv_y(): return 0.5 * (values[..., 2:, :] - values[..., :-2, :])]
    all_gather x8 -> x0, local copies, waits for them, and re-layouts: 24.7 us -> none  [fetch_flow(): return lax.all_gather(held_tile, 'mode', axis=2, tiled=True)]
    another operation x56, other arithmetic: 8.18 us -> 31.4 us  [tendency(): return jnp.stack([height_rate, zonal_rate, merid_rate], 1)]
    slice x208 -> x144, local copies, waits for them, and re-layouts: 49.1 us -> 53.2 us  [deriv_x(): return 0.5 * (jnp.roll(values, -1, -1) - jnp.roll(values, 1, -1))]
  transfers between devices with their start and end apart: 35 -> 43, of which waited for: 10 -> 18; matrix products, arithmetic and copies ran while one was open for 7% -> 10% of each run, Pallas kernels for 0% -> 0%
where the time goes in v1:
time: 586 us; the launch traced here: 580 us
  local copies, waits for them, and re-layouts  175 us (30%)
  starting transfers between devices  169 us (29%)
  waiting for transfers between devices  136 us (23%)
  other arithmetic  80.8 us (14%)
  loops' own time  17.9 us (3%)
    all_to_all x8, waiting for transfers between devices, swapped_in(): pieces = lax.all_to_all(pieces, axis, split_axis=0, concat_axis=0)  104 us
    ppermute x17, starting transfers between devices, padded(): lax.ppermute(tail, axis, [(i, (i + 1) % count) for i in range(ends)])  89.1 us
    slice x144, local copies, waits for them, and re-layouts, deriv_x(): return 0.5 * (jnp.roll(values, -1, -1) - jnp.roll(values, 1, -1))  53.2 us
    all_to_all x8, starting transfers between devices, swapped_in(): pieces = lax.all_to_all(pieces, axis, split_axis=0, concat_axis=0)  42.8 us
    ppermute x17, starting transfers between devices, padded(): lax.ppermute(head, axis, [((i + 1) % count, i) for i in range(ends)])  32.8 us
    another operation x56, other arithmetic, tendency(): return jnp.stack([height_rate, zonal_rate, merid_rate], 1)  31.4 us
    all_to_all x1, waiting for transfers between devices, on_device(): lax.all_to_all(final, 'mode', split_axis=3, concat_axis=0, tiled=True)  21.5 us
    unnamed x7, local copies, waits for them, and re-layouts  20.1 us
  transfers between devices with their start and end apart: 43, of which 18 were waited for; matrix products, arithmetic and copies ran while one was open for 10% of the time, Pallas kernels for 0%

profile of v1, /device:TPU:97, one launch (start us, length us, event | category | flops | bytes accessed | tf_op | source)
XLA Modules:
  0.0 580.3 jit_solution(18049364817378683403)
XLA Ops:
  0.9 5.3 collective-permute-start.4
  13.3 508.8 %while.13 = (s32[]{:T(128)}, f32[4,3,8,1024]{3,2,1,0:T(8,128)S(1)}, f32[8,1024]{1,0:T(8,128)}, s32[8]{0:T(128)}, f32[8,3,10,32]{3,1,2,0:T(4,128)}, /*index=5*/s32[]{:T(128)}, s32[]{:T(128)}, s32[]{:T(128)}, f32[]{:T(128)}) while((s32[]{:T(128)}, f32[4,3,8,1024]{3,2,1,0:T(8,128)S(1)}, f32[8,1024]{1,0:T(8,128)}, s32[8]{0:T(128)}, ...), condition=%wide.region_1.2_spmd, body=%wide.region_0.1_spmd.sunk | while | flops 5195781 | bytes 28583172 | solution.py:109
  15.2 4.9 collective-permute-start.1
  25.2 15.5 %all-to-all-start = ((f32[32,1,960]{2,1,0:T(1,128)}), f32[32,1,960]{2,1,0:T(1,128)S(1)}, u32[]{:S(2)}, u32[]{:S(2)}) async-start(f32[32,1,960]{2,1,0:T(1,128)} %reshape.94), calls=%async_computation | async-start | bytes 262144 | tf_op jit(solution)/shard_map/while/body/eval_jaxpr/all_to_all | solution.py:15
  44.3 13.8 %all-to-all-done = f32[32,1,960]{2,1,0:T(1,128)S(1)} async-done(((f32[32,1,960]{2,1,0:T(1,128)}), f32[32,1,960]{2,1,0:T(1,128)S(1)}, u32[]{:S(2)}, u32[]{:S(2)}) %all-to-all-start) | async-done | bytes 122912 | tf_op jit(solution)/shard_map/while/body/eval_jaxpr/all_to_all | solution.py:15
  79.3 4.7 collective-permute-start.3
  89.0 5.5 collective-permute-start.1
  107.1 12.7 %all-to-all-done = f32[32,1,960]{2,1,0:T(1,128)S(1)} async-done(((f32[32,1,960]{2,1,0:T(1,128)}), f32[32,1,960]{2,1,0:T(1,128)S(1)}, u32[]{:S(2)}, u32[]{:S(2)}) %all-to-all-start) | async-done | bytes 122912 | tf_op jit(solution)/shard_map/while/body/eval_jaxpr/all_to_all | solution.py:15
  140.8 6.1 %collective-permute-start.3 = (f32[4,3,1,1024]{3,2,0,1:T(1,128)S(1)}, f32[4,3,1,1024]{3,2,0,1:T(1,128)S(1)}, u32[]{:S(2)}, u32[]{:S(2)}) collective-permute-start(f32[4,3,1,1024]{3,2,0,1:T(1,128)S(1)} %get-tuple-element.313), channel_id=1, source_target_pairs={{0,1},{1,2},{2,3},{3,4},{4,5},{5,6},{6,7},{7,8},{8,9},{9,10},{10,1... | collective-permute-start | bytes 147464 | tf_op jit(solution)/shard_map/while/body/eval_jaxpr/ppermute | solution.py:27
  151.9 5.5 collective-permute-start.1
  169.9 13.2 %all-to-all-done = f32[32,1,960]{2,1,0:T(1,128)S(1)} async-done(((f32[32,1,960]{2,1,0:T(1,128)}), f32[32,1,960]{2,1,0:T(1,128)S(1)}, u32[]{:S(2)}, u32[]{:S(2)}) %all-to-all-start) | async-done | bytes 122912 | tf_op jit(solution)/shard_map/while/body/eval_jaxpr/all_to_all | solution.py:15
  204.1 5.6 collective-permute-start.3
  214.8 5.5 collective-permute-start.1
  232.8 12.7 %all-to-all-done = f32[32,1,960]{2,1,0:T(1,128)S(1)} async-done(((f32[32,1,960]{2,1,0:T(1,128)}), f32[32,1,960]{2,1,0:T(1,128)S(1)}, u32[]{:S(2)}, u32[]{:S(2)}) %all-to-all-start) | async-done | bytes 122912 | tf_op jit(solution)/shard_map/while/body/eval_jaxpr/all_to_all | solution.py:15
  266.5 4.9 collective-permute-start.3
  276.5 5.5 collective-permute-start.1
  294.5 13.4 %all-to-all-done = f32[32,1,960]{2,1,0:T(1,128)S(1)} async-done(((f32[32,1,960]{2,1,0:T(1,128)}), f32[32,1,960]{2,1,0:T(1,128)S(1)}, u32[]{:S(2)}, u32[]{:S(2)}) %all-to-all-start) | async-done | bytes 122912 | tf_op jit(solution)/shard_map/while/body/eval_jaxpr/all_to_all | solution.py:15
  328.9 4.9 collective-permute-start.3
  338.8 5.5 collective-permute-start.1
  356.8 12.7 %all-to-all-done = f32[32,1,960]{2,1,0:T(1,128)S(1)} async-done(((f32[32,1,960]{2,1,0:T(1,128)}), f32[32,1,960]{2,1,0:T(1,128)S(1)}, u32[]{:S(2)}, u32[]{:S(2)}) %all-to-all-start) | async-done | bytes 122912 | tf_op jit(solution)/shard_map/while/body/eval_jaxpr/all_to_all | solution.py:15
  390.6 4.9 collective-permute-start.3
  400.4 5.5 collective-permute-start.1
  418.5 12.7 %all-to-all-done = f32[32,1,960]{2,1,0:T(1,128)S(1)} async-done(((f32[32,1,960]{2,1,0:T(1,128)}), f32[32,1,960]{2,1,0:T(1,128)S(1)}, u32[]{:S(2)}, u32[]{:S(2)}) %all-to-all-start) | async-done | bytes 122912 | tf_op jit(solution)/shard_map/while/body/eval_jaxpr/all_to_all | solution.py:15
  452.2 4.9 collective-permute-start.3
  462.0 5.5 collective-permute-start.1
  480.4 12.7 %all-to-all-done = f32[32,1,960]{2,1,0:T(1,128)S(1)} async-done(((f32[32,1,960]{2,1,0:T(1,128)}), f32[32,1,960]{2,1,0:T(1,128)S(1)}, u32[]{:S(2)}, u32[]{:S(2)}) %all-to-all-start) | async-done | bytes 122912 | tf_op jit(solution)/shard_map/while/body/eval_jaxpr/all_to_all | solution.py:15
  514.2 4.9 collective-permute-start.3
  522.0 4.5 copy.87
  526.6 9.3 %reshape.90 = f32[32,1,3072]{2,1,0:T(1,128)} reshape(f32[1024,3,4,8]{3,2,1,0:T(4,128)} %bitcast.118) | data formatting | bytes 786432
  540.0 21.5 %all-to-all-done.1 = f32[32,1,3072]{2,1,0:T(1,128)S(1)} async-done(((f32[32,1,3072]{2,1,0:T(1,128)}), f32[32,1,3072]{2,1,0:T(1,128)S(1)}, u32[]{:S(2)}, u32[]{:S(2)}) %all-to-all-start.1) | async-done | bytes 393248 | tf_op jit(solution)/shard_map/all_to_all | solution.py:111
  563.6 9.2 %reshape.91 = f32[1024,3,4,8]{3,2,1,0:T(4,128)} reshape(f32[32,3072]{1,0:T(8,128)S(1)} %reduce.1) | data formatting | bytes 786432
  572.8 5.6 copy.88
  (594 shorter events, 303.8 us)
Async XLA Ops:
  0.9 9.6 %collective-permute-start.4 = (f32[8,3,1,32]{3,1,2,0:T(4,128)S(1)}, f32[8,3,1,32]{3,1,2,0:T(4,128)S(1)}, u32[]{:S(2)}, u32[]{:S(2)}) collective-permute-start(f32[8,3,1,32]{3,1,2,0:T(4,128)S(1)} %get-tuple-element.177), channel_id=1, source_target_pairs={{0,1},{1,2},{2,3},{3,4},{4,5},{5,6},{6,7},{7,8},{8,9},{9,10},{10,1... | collective-permute-start | bytes 9224 | tf_op jit(solution)/shard_map/ppermute | solution.py:27
  13.3 27.4 %collective-permute-start = (f32[4,3,1,1024]{3,2,0,1:T(1,128)S(1)}, f32[4,3,1,1024]{3,2,0,1:T(1,128)S(1)}, u32[]{:S(2)}, u32[]{:S(2)}) collective-permute-start(f32[4,3,1,1024]{3,2,0,1:T(1,128)S(1)} %get-tuple-element.273), channel_id=1, source_target_pairs={{1,0},{2,1},{3,2},{4,3},{5,4},{6,5},{7,6},{8,7},{9,8},{10,9},{11,1... | collective-permute-start | bytes 147464 | tf_op jit(solution)/shard_map/while/body/eval_jaxpr/ppermute | solution.py:29
  15.2 25.5 %collective-permute-start.1 = (f32[4,3,1,1024]{3,2,0,1:T(1,128)S(1)}, f32[4,3,1,1024]{3,2,0,1:T(1,128)S(1)}, u32[]{:S(2)}, u32[]{:S(2)}) collective-permute-start(f32[4,3,1,1024]{3,2,0,1:T(1,128)S(1)} %get-tuple-element.274), channel_id=1, source_target_pairs={{0,1},{1,2},{2,3},{3,4},{4,5},{5,6},{6,7},{7,8},{8,9},{9,10},{10,1... | collective-permute-start | bytes 147464 | tf_op jit(solution)/shard_map/while/body/eval_jaxpr/ppermute | solution.py:27
  25.2 32.9 %all-to-all-start = ((f32[32,1,960]{2,1,0:T(1,128)}), f32[32,1,960]{2,1,0:T(1,128)S(1)}, u32[]{:S(2)}, u32[]{:S(2)}) async-start(f32[32,1,960]{2,1,0:T(1,128)} %reshape.94), calls=%async_computation | async-start | bytes 262144 | tf_op jit(solution)/shard_map/while/body/eval_jaxpr/all_to_all | solution.py:15
  77.2 6.8 %collective-permute-start.2 = (f32[4,3,1,1024]{3,2,0,1:T(1,128)S(1)}, f32[4,3,1,1024]{3,2,0,1:T(1,128)S(1)}, u32[]{:S(2)}, u32[]{:S(2)}) collective-permute-start(f32[4,3,1,1024]{3,2,0,1:T(1,128)S(1)} %get-tuple-element.312), channel_id=1, source_target_pairs={{1,0},{2,1},{3,2},{4,3},{5,4},{6,5},{7,6},{8,7},{9,8},{10,9},{11,1... | collective-permute-start | bytes 147464 | tf_op jit(solution)/shard_map/while/body/eval_jaxpr/ppermute | solution.py:29
  87.1 16.4 %collective-permute-start = (f32[4,3,1,1024]{3,2,0,1:T(1,128)S(1)}, f32[4,3,1,1024]{3,2,0,1:T(1,128)S(1)}, u32[]{:S(2)}, u32[]{:S(2)}) collective-permute-start(f32[4,3,1,1024]{3,2,0,1:T(1,128)S(1)} %get-tuple-element.273), channel_id=1, source_target_pairs={{1,0},{2,1},{3,2},{4,3},{5,4},{6,5},{7,6},{8,7},{9,8},{10,9},{11,1... | collective-permute-start | bytes 147464 | tf_op jit(solution)/shard_map/while/body/eval_jaxpr/ppermute | solution.py:29
  89.0 14.5 %collective-permute-start.1 = (f32[4,3,1,1024]{3,2,0,1:T(1,128)S(1)}, f32[4,3,1,1024]{3,2,0,1:T(1,128)S(1)}, u32[]{:S(2)}, u32[]{:S(2)}) collective-permute-start(f32[4,3,1,1024]{3,2,0,1:T(1,128)S(1)} %get-tuple-element.274), channel_id=1, source_target_pairs={{0,1},{1,2},{2,3},{3,4},{4,5},{5,6},{6,7},{7,8},{8,9},{9,10},{10,1... | collective-permute-start | bytes 147464 | tf_op jit(solution)/shard_map/while/body/eval_jaxpr/ppermute | solution.py:27
  99.6 20.1 %all-to-all-start = ((f32[32,1,960]{2,1,0:T(1,128)}), f32[32,1,960]{2,1,0:T(1,128)S(1)}, u32[]{:S(2)}, u32[]{:S(2)}) async-start(f32[32,1,960]{2,1,0:T(1,128)} %reshape.94), calls=%async_computation | async-start | bytes 262144 | tf_op jit(solution)/shard_map/while/body/eval_jaxpr/all_to_all | solution.py:15
  138.8 8.0 %collective-permute-start.2 = (f32[4,3,1,1024]{3,2,0,1:T(1,128)S(1)}, f32[4,3,1,1024]{3,2,0,1:T(1,128)S(1)}, u32[]{:S(2)}, u32[]{:S(2)}) collective-permute-start(f32[4,3,1,1024]{3,2,0,1:T(1,128)S(1)} %get-tuple-element.312), channel_id=1, source_target_pairs={{1,0},{2,1},{3,2},{4,3},{5,4},{6,5},{7,6},{8,7},{9,8},{10,9},{11,1... | collective-permute-start | bytes 147464 | tf_op jit(solution)/shard_map/while/body/eval_jaxpr/ppermute | solution.py:29
  140.8 7.3 %collective-permute-start.3 = (f32[4,3,1,1024]{3,2,0,1:T(1,128)S(1)}, f32[4,3,1,1024]{3,2,0,1:T(1,128)S(1)}, u32[]{:S(2)}, u32[]{:S(2)}) collective-permute-start(f32[4,3,1,1024]{3,2,0,1:T(1,128)S(1)} %get-tuple-element.313), channel_id=1, source_target_pairs={{0,1},{1,2},{2,3},{3,4},{4,5},{5,6},{6,7},{7,8},{8,9},{9,10},{10,1... | collective-permute-start | bytes 147464 | tf_op jit(solution)/shard_map/while/body/eval_jaxpr/ppermute | solution.py:27
  150.0 16.4 %collective-permute-start = (f32[4,3,1,1024]{3,2,0,1:T(1,128)S(1)}, f32[4,3,1,1024]{3,2,0,1:T(1,128)S(1)}, u32[]{:S(2)}, u32[]{:S(2)}) collective-permute-start(f32[4,3,1,1024]{3,2,0,1:T(1,128)S(1)} %get-tuple-element.273), channel_id=1, source_target_pairs={{1,0},{2,1},{3,2},{4,3},{5,4},{6,5},{7,6},{8,7},{9,8},{10,9},{11,1... | collective-permute-start | bytes 147464 | tf_op jit(solution)/shard_map/while/body/eval_jaxpr/ppermute | solution.py:29
  151.9 14.5 %collective-permute-start.1 = (f32[4,3,1,1024]{3,2,0,1:T(1,128)S(1)}, f32[4,3,1,1024]{3,2,0,1:T(1,128)S(1)}, u32[]{:S(2)}, u32[]{:S(2)}) collective-permute-start(f32[4,3,1,1024]{3,2,0,1:T(1,128)S(1)} %get-tuple-element.274), channel_id=1, source_target_pairs={{0,1},{1,2},{2,3},{3,4},{4,5},{5,6},{6,7},{7,8},{8,9},{9,10},{10,1... | collective-permute-start | bytes 147464 | tf_op jit(solution)/shard_map/while/body/eval_jaxpr/ppermute | solution.py:27
  162.5 20.6 %all-to-all-start = ((f32[32,1,960]{2,1,0:T(1,128)}), f32[32,1,960]{2,1,0:T(1,128)S(1)}, u32[]{:S(2)}, u32[]{:S(2)}) async-start(f32[32,1,960]{2,1,0:T(1,128)} %reshape.94), calls=%async_computation | async-start | bytes 262144 | tf_op jit(solution)/shard_map/while/body/eval_jaxpr/all_to_all | solution.py:15
  202.2 7.5 %collective-permute-start.2 = (f32[4,3,1,1024]{3,2,0,1:T(1,128)S(1)}, f32[4,3,1,1024]{3,2,0,1:T(1,128)S(1)}, u32[]{:S(2)}, u32[]{:S(2)}) collective-permute-start(f32[4,3,1,1024]{3,2,0,1:T(1,128)S(1)} %get-tuple-element.312), channel_id=1, source_target_pairs={{1,0},{2,1},{3,2},{4,3},{5,4},{6,5},{7,6},{8,7},{9,8},{10,9},{11,1... | collective-permute-start | bytes 147464 | tf_op jit(solution)/shard_map/while/body/eval_jaxpr/ppermute | solution.py:29
  212.8 16.4 %collective-permute-start = (f32[4,3,1,1024]{3,2,0,1:T(1,128)S(1)}, f32[4,3,1,1024]{3,2,0,1:T(1,128)S(1)}, u32[]{:S(2)}, u32[]{:S(2)}) collective-permute-start(f32[4,3,1,1024]{3,2,0,1:T(1,128)S(1)} %get-tuple-element.273), channel_id=1, source_target_pairs={{1,0},{2,1},{3,2},{4,3},{5,4},{6,5},{7,6},{8,7},{9,8},{10,9},{11,1... | collective-permute-start | bytes 147464 | tf_op jit(solution)/shard_map/while/body/eval_jaxpr/ppermute | solution.py:29
  214.8 14.5 %collective-permute-start.1 = (f32[4,3,1,1024]{3,2,0,1:T(1,128)S(1)}, f32[4,3,1,1024]{3,2,0,1:T(1,128)S(1)}, u32[]{:S(2)}, u32[]{:S(2)}) collective-permute-start(f32[4,3,1,1024]{3,2,0,1:T(1,128)S(1)} %get-tuple-element.274), channel_id=1, source_target_pairs={{0,1},{1,2},{2,3},{3,4},{4,5},{5,6},{6,7},{7,8},{8,9},{9,10},{10,1... | collective-permute-start | bytes 147464 | tf_op jit(solution)/shard_map/while/body/eval_jaxpr/ppermute | solution.py:27
  225.3 20.1 %all-to-all-start = ((f32[32,1,960]{2,1,0:T(1,128)}), f32[32,1,960]{2,1,0:T(1,128)S(1)}, u32[]{:S(2)}, u32[]{:S(2)}) async-start(f32[32,1,960]{2,1,0:T(1,128)} %reshape.94), calls=%async_computation | async-start | bytes 262144 | tf_op jit(solution)/shard_map/while/body/eval_jaxpr/all_to_all | solution.py:15
  264.6 6.9 %collective-permute-start.2 = (f32[4,3,1,1024]{3,2,0,1:T(1,128)S(1)}, f32[4,3,1,1024]{3,2,0,1:T(1,128)S(1)}, u32[]{:S(2)}, u32[]{:S(2)}) collective-permute-start(f32[4,3,1,1024]{3,2,0,1:T(1,128)S(1)} %get-tuple-element.312), channel_id=1, source_target_pairs={{1,0},{2,1},{3,2},{4,3},{5,4},{6,5},{7,6},{8,7},{9,8},{10,9},{11,1... | collective-permute-start | bytes 147464 | tf_op jit(solution)/shard_map/while/body/eval_jaxpr/ppermute | solution.py:29
  274.5 16.4 %collective-permute-start = (f32[4,3,1,1024]{3,2,0,1:T(1,128)S(1)}, f32[4,3,1,1024]{3,2,0,1:T(1,128)S(1)}, u32[]{:S(2)}, u32[]{:S(2)}) collective-permute-start(f32[4,3,1,1024]{3,2,0,1:T(1,128)S(1)} %get-tuple-element.273), channel_id=1, source_target_pairs={{1,0},{2,1},{3,2},{4,3},{5,4},{6,5},{7,6},{8,7},{9,8},{10,9},{11,1... | collective-permute-start | bytes 147464 | tf_op jit(solution)/shard_map/while/body/eval_jaxpr/ppermute | solution.py:29
  276.5 14.5 %collective-permute-start.1 = (f32[4,3,1,1024]{3,2,0,1:T(1,128)S(1)}, f32[4,3,1,1024]{3,2,0,1:T(1,128)S(1)}, u32[]{:S(2)}, u32[]{:S(2)}) collective-permute-start(f32[4,3,1,1024]{3,2,0,1:T(1,128)S(1)} %get-tuple-element.274), channel_id=1, source_target_pairs={{0,1},{1,2},{2,3},{3,4},{4,5},{5,6},{6,7},{7,8},{8,9},{9,10},{10,1... | collective-permute-start | bytes 147464 | tf_op jit(solution)/shard_map/while/body/eval_jaxpr/ppermute | solution.py:27
  287.0 20.8 %all-to-all-start = ((f32[32,1,960]{2,1,0:T(1,128)}), f32[32,1,960]{2,1,0:T(1,128)S(1)}, u32[]{:S(2)}, u32[]{:S(2)}) async-start(f32[32,1,960]{2,1,0:T(1,128)} %reshape.94), calls=%async_computation | async-start | bytes 262144 | tf_op jit(solution)/shard_map/while/body/eval_jaxpr/all_to_all | solution.py:15
  327.0 6.8 %collective-permute-start.2 = (f32[4,3,1,1024]{3,2,0,1:T(1,128)S(1)}, f32[4,3,1,1024]{3,2,0,1:T(1,128)S(1)}, u32[]{:S(2)}, u32[]{:S(2)}) collective-permute-start(f32[4,3,1,1024]{3,2,0,1:T(1,128)S(1)} %get-tuple-element.312), channel_id=1, source_target_pairs={{1,0},{2,1},{3,2},{4,3},{5,4},{6,5},{7,6},{8,7},{9,8},{10,9},{11,1... | collective-permute-start | bytes 147464 | tf_op jit(solution)/shard_map/while/body/eval_jaxpr/ppermute | solution.py:29
  336.9 16.4 %collective-permute-start = (f32[4,3,1,1024]{3,2,0,1:T(1,128)S(1)}, f32[4,3,1,1024]{3,2,0,1:T(1,128)S(1)}, u32[]{:S(2)}, u32[]{:S(2)}) collective-permute-start(f32[4,3,1,1024]{3,2,0,1:T(1,128)S(1)} %get-tuple-element.273), channel_id=1, source_target_pairs={{1,0},{2,1},{3,2},{4,3},{5,4},{6,5},{7,6},{8,7},{9,8},{10,9},{11,1... | collective-permute-start | bytes 147464 | tf_op jit(solution)/shard_map/while/body/eval_jaxpr/ppermute | solution.py:29
  338.8 14.5 %collective-permute-start.1 = (f32[4,3,1,1024]{3,2,0,1:T(1,128)S(1)}, f32[4,3,1,1024]{3,2,0,1:T(1,128)S(1)}, u32[]{:S(2)}, u32[]{:S(2)}) collective-permute-start(f32[4,3,1,1024]{3,2,0,1:T(1,128)S(1)} %get-tuple-element.274), channel_id=1, source_target_pairs={{0,1},{1,2},{2,3},{3,4},{4,5},{5,6},{6,7},{7,8},{8,9},{9,10},{10,1... | collective-permute-start | bytes 147464 | tf_op jit(solution)/shard_map/while/body/eval_jaxpr/ppermute | solution.py:27
  349.4 20.1 %all-to-all-start = ((f32[32,1,960]{2,1,0:T(1,128)}), f32[32,1,960]{2,1,0:T(1,128)S(1)}, u32[]{:S(2)}, u32[]{:S(2)}) async-start(f32[32,1,960]{2,1,0:T(1,128)} %reshape.94), calls=%async_computation | async-start | bytes 262144 | tf_op jit(solution)/shard_map/while/body/eval_jaxpr/all_to_all | solution.py:15
  398.5 16.4 %collective-permute-start = (f32[4,3,1,1024]{3,2,0,1:T(1,128)S(1)}, f32[4,3,1,1024]{3,2,0,1:T(1,128)S(1)}, u32[]{:S(2)}, u32[]{:S(2)}) collective-permute-start(f32[4,3,1,1024]{3,2,0,1:T(1,128)S(1)} %get-tuple-element.273), channel_id=1, source_target_pairs={{1,0},{2,1},{3,2},{4,3},{5,4},{6,5},{7,6},{8,7},{9,8},{10,9},{11,1... | collective-permute-start | bytes 147464 | tf_op jit(solution)/shard_map/while/body/eval_jaxpr/ppermute | solution.py:29
  400.4 14.5 %collective-permute-start.1 = (f32[4,3,1,1024]{3,2,0,1:T(1,128)S(1)}, f32[4,3,1,1024]{3,2,0,1:T(1,128)S(1)}, u32[]{:S(2)}, u32[]{:S(2)}) collective-permute-start(f32[4,3,1,1024]{3,2,0,1:T(1,128)S(1)} %get-tuple-element.274), channel_id=1, source_target_pairs={{0,1},{1,2},{2,3},{3,4},{4,5},{5,6},{6,7},{7,8},{8,9},{9,10},{10,1... | collective-permute-start | bytes 147464 | tf_op jit(solution)/shard_map/while/body/eval_jaxpr/ppermute | solution.py:27
  411.0 20.1 %all-to-all-start = ((f32[32,1,960]{2,1,0:T(1,128)}), f32[32,1,960]{2,1,0:T(1,128)S(1)}, u32[]{:S(2)}, u32[]{:S(2)}) async-start(f32[32,1,960]{2,1,0:T(1,128)} %reshape.94), calls=%async_computation | async-start | bytes 262144 | tf_op jit(solution)/shard_map/while/body/eval_jaxpr/all_to_all | solution.py:15
  460.1 16.7 %collective-permute-start = (f32[4,3,1,1024]{3,2,0,1:T(1,128)S(1)}, f32[4,3,1,1024]{3,2,0,1:T(1,128)S(1)}, u32[]{:S(2)}, u32[]{:S(2)}) collective-permute-start(f32[4,3,1,1024]{3,2,0,1:T(1,128)S(1)} %get-tuple-element.273), channel_id=1, source_target_pairs={{1,0},{2,1},{3,2},{4,3},{5,4},{6,5},{7,6},{8,7},{9,8},{10,9},{11,1... | collective-permute-start | bytes 147464 | tf_op jit(solution)/shard_map/while/body/eval_jaxpr/ppermute | solution.py:29
  462.0 14.8 %collective-permute-start.1 = (f32[4,3,1,1024]{3,2,0,1:T(1,128)S(1)}, f32[4,3,1,1024]{3,2,0,1:T(1,128)S(1)}, u32[]{:S(2)}, u32[]{:S(2)}) collective-permute-start(f32[4,3,1,1024]{3,2,0,1:T(1,128)S(1)} %get-tuple-element.274), channel_id=1, source_target_pairs={{0,1},{1,2},{2,3},{3,4},{4,5},{5,6},{6,7},{7,8},{8,9},{9,10},{10,1... | collective-permute-start | bytes 147464 | tf_op jit(solution)/shard_map/while/body/eval_jaxpr/ppermute | solution.py:27
  472.6 20.5 %all-to-all-start = ((f32[32,1,960]{2,1,0:T(1,128)}), f32[32,1,960]{2,1,0:T(1,128)S(1)}, u32[]{:S(2)}, u32[]{:S(2)}) async-start(f32[32,1,960]{2,1,0:T(1,128)} %reshape.94), calls=%async_computation | async-start | bytes 262144 | tf_op jit(solution)/shard_map/while/body/eval_jaxpr/all_to_all | solution.py:15
  535.9 25.6 %all-to-all-start.1 = ((f32[32,1,3072]{2,1,0:T(1,128)}), f32[32,1,3072]{2,1,0:T(1,128)S(1)}, u32[]{:S(2)}, u32[]{:S(2)}) async-start(f32[32,1,3072]{2,1,0:T(1,128)} %reshape.90), calls=%async_computation.1 | async-start | bytes 786432 | tf_op jit(solution)/shard_map/all_to_all | solution.py:111
  (61 other events, 772.9 us)
